TPU v7x, 32 devices: a whole 2x2x4 slice. The times are simulated.
32 devices in a mesh: seq: 8 (over z, x), tp: 4 (over y, core).
Axes of the slice: x: 2, y: 2, z: 4, core: 2. Of those that a mesh axis runs over, the one named last changes fastest.
Arguments:
- teacher_hidden: bfloat16 [1024, 4096], P('seq', 'tp'), may hold values from -6 to 6
- proj_weight: bfloat16 [4096, 3584], P('tp'), may hold values from -0.09375 to 0.09375
- student_in: bfloat16 [1280, 3584], P('seq'), may hold values from -6 to 6
- norm_gain: float32 [3584], replicated, may hold values from 0.25 to 1.75
- w_query: bfloat16 [3584, 1024], P(None, 'tp')
- w_keyval: bfloat16 [3584, 1024], P(None, 'tp')
- w_out: bfloat16 [1024, 3584], P('tp'), may hold values from -0.1875 to 0.1875
- row_offsets: int32 [8], P('seq'), may hold values from 0 to 864, as said below
- row_counts: int32 [8], P('seq'), may hold values from 96 to 160, as said below
- doc_start: int32 [1280], P('seq'), may hold values from 0 to 159, as said below
Outputs:
- student_out: bfloat16 [1280, 3584], P('seq')
- grad_in: bfloat16 [1280, 3584], P(('seq', 'tp'))
Inputs may be any that keep to these rules, and one draw needn't show every extreme that they name: Block s holds the tokens row_offsets[s] to row_offsets[s] + row_counts[s] - 1 in its first slots; row_offsets[0] = 0, for s >= 1 row_offsets[s] lies between s * 128 - 128 // 4 and s * 128 - 1, and row_offsets[s] + row_counts[s] = row_offsets[s + 1], the last block ending at 1024. `row_counts`: see row_offsets; some block holds 160 tokens and some 128 - 128 // 4. Within a block doc_start never falls, doc_start[p] <= p, documents lie whole in one block, and the slots from row_counts onward start a new document at row_counts.
All inputs are finite; a program needn't handle non-finite values.
Results may differ from a plain program's by a relative error of at most 0.028.
The roundings to bfloat16 on the way count: a program that leaves them out, or rounds other values in their place, can miss the bound.
Values may be sent and summed in bfloat16 or wider, within the bound.
A program may use at most 64 MiB of HBM per device.

v0:
```python
import math

import jax
import jax.numpy as jnp
from jax import lax
from jax.sharding import PartitionSpec as P

HD = 128
QPK = 2


epsilon = 1e-06


def from_behind(block, axis, distance):
    devices = range(lax.axis_size(axis))
    route = [(i - distance, i) for i in devices if i - distance in devices]
    return lax.ppermute(block, axis, route)


def body(
    teacher_hidden,
    proj_weight,
    student_in,
    norm_gain,
    w_query,
    w_keyval,
    w_out,
    row_offsets,
    row_counts,
    doc_start,
):
    scale = 1.0 / math.sqrt(HD)
    tokens_here = teacher_hidden.shape[0]
    quarter = tokens_here // 4
    slots_here = student_in.shape[0]
    width = student_in.shape[1]
    start = row_offsets[0] - lax.axis_index("seq") * tokens_here + quarter
    count = row_counts[0]
    xf = student_in.astype(jnp.float32)
    inv = lax.rsqrt(jnp.mean(xf * xf, axis=1, keepdims=True) + epsilon)
    normed = (xf * inv * norm_gain).astype(jnp.bfloat16)
    query = (
        jnp.dot(normed, w_query, preferred_element_type=jnp.float32)
        .astype(jnp.bfloat16)
        .reshape(slots_here, QPK, HD)
    )
    keyval = (
        jnp.dot(normed, w_keyval, preferred_element_type=jnp.float32)
        .astype(jnp.bfloat16)
        .reshape(slots_here, 2, HD)
    )
    keys = keyval[:, 0, :]
    values = keyval[:, 1, :]
    slots = jnp.arange(slots_here, dtype=jnp.int32)
    allowed = (slots[None, :] >= doc_start[:, None]) & (slots[None, :] <= slots[:, None])
    scores = jnp.einsum("peh,kh->epk", query, keys, preferred_element_type=jnp.float32) * scale
    scores = jnp.where(allowed[None], scores, -jnp.inf)
    top = jnp.max(scores, axis=-1, keepdims=True)
    expo = jnp.exp(scores - top)
    probs = expo / jnp.sum(expo, axis=-1, keepdims=True)
    probs_b = probs.astype(jnp.bfloat16)
    attn = jnp.einsum("epk,kh->peh", probs_b, values, preferred_element_type=jnp.float32).astype(
        jnp.bfloat16
    )
    attn = attn.reshape(slots_here, QPK * HD)
    branch_part = jnp.dot(attn, w_out, preferred_element_type=jnp.float32).astype(jnp.bfloat16)
    earlier = from_behind(teacher_hidden[tokens_here - quarter :], "seq", 1)
    features = jnp.concatenate(
        [earlier, teacher_hidden, jnp.zeros((quarter, teacher_hidden.shape[1]), jnp.bfloat16)],
        axis=0,
    )
    picked = lax.dynamic_slice_in_dim(features, start, slots_here, 0)
    projected = jnp.dot(picked, proj_weight, preferred_element_type=jnp.float32).astype(
        jnp.bfloat16
    )
    goal_sum, branch = (
        lax.psum(projected, "tp").astype(jnp.float32),
        lax.psum(branch_part, "tp").astype(jnp.float32),
    )
    goal = goal_sum.astype(jnp.bfloat16)
    student_out = (xf + branch).astype(jnp.bfloat16)
    yf = student_out.astype(jnp.float32)
    tf = goal.astype(jnp.float32)
    live = (slots < count).astype(jnp.float32)[:, None]
    asum = jnp.sum(yf * yf, axis=1, keepdims=True) + epsilon
    bsum = jnp.sum(tf * tf, axis=1, keepdims=True) + epsilon
    both = lax.rsqrt(asum * bsum)
    cosv = jnp.sum(yf * tf, axis=1, keepdims=True) * both
    dy = -math.sqrt(width) * live * (tf * both - cosv * yf / asum)
    dy_b = dy.astype(jnp.bfloat16)
    d_attn = lax.dot_general(
        dy_b, w_out, (((1,), (1,)), ((), ())), preferred_element_type=jnp.float32
    ).astype(jnp.bfloat16)
    d_out = d_attn.reshape(slots_here, QPK, HD)
    d_values = jnp.einsum("epk,peh->kh", probs_b, d_out, preferred_element_type=jnp.float32).astype(
        jnp.bfloat16
    )
    dprob = jnp.einsum("peh,kh->epk", d_out, values, preferred_element_type=jnp.float32)
    dscore = probs * (dprob - jnp.sum(dprob * probs, axis=-1, keepdims=True)) * scale
    dscore_b = dscore.astype(jnp.bfloat16)
    d_query = jnp.einsum("epk,kh->peh", dscore_b, keys, preferred_element_type=jnp.float32).astype(
        jnp.bfloat16
    )
    d_query = d_query.reshape(slots_here, QPK * HD)
    d_keys = jnp.einsum("epk,peh->kh", dscore_b, query, preferred_element_type=jnp.float32).astype(
        jnp.bfloat16
    )
    d_keyval = jnp.stack([d_keys, d_values], axis=1).reshape(slots_here, 2 * HD)
    own_rows = slots_here // lax.axis_size("tp")
    total = lax.dot_general(
        d_query, w_query, (((1,), (1,)), ((), ())), preferred_element_type=jnp.float32
    )
    d_normed = lax.psum_scatter(
        (
            total
            + lax.dot_general(
                d_keyval, w_keyval, (((1,), (1,)), ((), ())), preferred_element_type=jnp.float32
            )
        ).astype(jnp.bfloat16),
        "tp",
        scatter_dimension=0,
        tiled=True,
    ).astype(jnp.float32)
    first_row = lax.axis_index("tp") * own_rows
    x_own = lax.dynamic_slice_in_dim(xf, first_row, own_rows, 0)
    inv_own = lax.dynamic_slice_in_dim(inv, first_row, own_rows, 0)
    dy_own = lax.dynamic_slice_in_dim(dy, first_row, own_rows, 0)
    upper = d_normed * norm_gain
    dx = inv_own * upper - x_own * inv_own * inv_own * inv_own * jnp.mean(
        upper * x_own, axis=1, keepdims=True
    )
    grad_in = (dy_own + dx).astype(jnp.bfloat16)
    return (student_out, grad_in)


def solution(mesh):
    in_specs = (
        P("seq", "tp"),
        P("tp", None),
        P("seq", None),
        P(),
        P(None, "tp"),
        P(None, "tp"),
        P("tp", None),
        P("seq"),
        P("seq"),
        P("seq"),
    )
    out_specs = (P("seq", None), P(("seq", "tp"), None))
    return jax.shard_map(body, mesh=mesh, in_specs=in_specs, out_specs=out_specs, check_vma=False)
```

profile of v0, /device:TPU:9, one launch (start us, length us, event | category | flops | bytes accessed | tf_op | source)
XLA Modules:
  0.0 133.0 jit_solution(17931543722018722381)
XLA Ops:
  7.2 0.0 copy-start
  7.2 0.0 all-reduce.3.cloned.1.call-start
  7.2 1.0 slice.11
  8.2 3.1 %collective-permute-start = (bf16[32,1024]{1,0:T(8,128)(2,1)S(1)}, bf16[32,1024]{1,0:T(8,128)(2,1)}, u32[]{:S(2)}, u32[]{:S(2)}) collective-permute-start(bf16[32,1024]{1,0:T(8,128)(2,1)S(1)} %slice.11), channel_id=1, source_target_pairs={{0,4},{4,8},{8,12},{12,16},{16,20},{20,24},{24,28},{1,5},{5,9},{9,... | collective-permute-start | bytes 196616 | tf_op jit(solution)/shard_map/ppermute | solution.py:18
  12.0 0.0 copy-start.2
  12.0 0.0 copy-start.5
  12.0 0.0 copy-start.7
  12.0 1.7 %multiply_reduce_fusion = f32[160]{0:T(256)S(1)} fusion(bf16[160,3584]{1,0:T(8,128)(2,1)} %param.12), kind=kLoop, calls=%fused_computation.19 | loop fusion | flops 1720160 | bytes 1147520 | tf_op jit(solution)/shard_map/reduce_sum | solution.py:41
  13.7 0.7 fusion.42
  14.5 3.0 %fusion.24 = bf16[20,2,8,128]{3,2,1,0:T(8,128)(2,1)} fusion(bf16[3584,256]{1,0:T(8,128)(2,1)} %param.14, bf16[160,3584]{1,0:T(8,128)(2,1)} %param.12, f32[3584]{0:T(1024)} %param.13, f32[160]{0:T(256)S(1)} %add_rsqrt_fusion), kind=kOutput, calls=%fused_computation.39 | convolution fusion | flops 295936000 | bytes 3078784 | tf_op jit(solution)/shard_map/dot_general | solution.py:44
  17.5 0.0 copy-done.2
  17.5 0.0 copy-done.5
  17.5 0.0 copy-done.7
  17.5 0.5 convolution_convert_fusion.3
  18.0 0.1 fusion.74
  18.2 1.9 %fusion.75 = (f32[2,160]{1,0:T(2,128)S(1)}, f32[2,160,160]{1,2,0:T(8,128)}) fusion(pred[160,160]{0,1:T(8,128)(4,1)S(1)} %fusion.42, bf16[20,2,8,128]{3,2,1,0:T(8,128)(2,1)} %fusion.24, bf16[160,1,128]{2,1,0:T(2,128)(2,1)S(1)} %get-tuple-element.10), kind=kOutput, calls=%fused_computation.101 | convolution fusion | flops 13312159 | bytes 354560 | tf_op jit(solution)/shard_map/sub | solution.py:60
  20.1 0.0 copy-start.9
  20.1 1.3 fusion.22
  21.3 0.0 copy-done
  21.4 1.5 %convolution_convert_fusion.1 = bf16[160,3584]{1,0:T(8,128)(2,1)} fusion(bf16[256,3584]{1,0:T(8,128)(2,1)S(1)} %copy-done, bf16[2,20,8,128]{3,2,1,0:T(8,128)(2,1)S(1)} %fusion.22), kind=kOutput, calls=%fused_computation.5 | convolution fusion | flops 294174720 | bytes 3063808 | tf_op jit(solution)/shard_map/dot_general | solution.py:67
  22.8 0.1 pad_dynamic-slice_fusion.3
  22.9 0.0 collective-permute-done
  22.9 0.0 copy-done.9
  22.9 5.6 %convolution_convert_fusion = bf16[160,3584]{1,0:T(8,128)(2,1)} fusion(bf16[1024,3584]{1,0:T(8,128)(2,1)} %param.11, s32[]{:T(128)S(6)} %select_n.13, bf16[32,1024]{1,0:T(8,128)(2,1)} %collective-permute-done, bf16[128,1024]{1,0:T(8,128)(2,1)S(1)} %copy-done.9, bf16[160]{0:T(256)(128)(2,1)S(1)} %pad_dynamic-slice_fusion.3), kind=kOutput, calls=%fused_computation.4 | convolution fusion | flops 1175961600 | bytes 8814916 | tf_op jit(solution)/shard_map/dot_general | solution.py:74
  28.5 0.0 all-reduce.3.cloned.1.call-update
  28.5 0.0 reduce-scatter.2.cloned.1.call-start
  29.2 54.7 %all-reduce.3.cloned.1.call-done = (bf16[160,3584]{1,0:T(8,128)(2,1)}, bf16[160,3584]{1,0:T(8,128)(2,1)}) async-done(((bf16[160,3584]{1,0:T(8,128)(2,1)}, bf16[160,3584]{1,0:T(8,128)(2,1)}), (bf16[160,3584]{1,0:T(8,128)(2,1)}, bf16[160,3584]{1,0:T(8,128)(2,1)})) %all-reduce.3.cloned.1.call-update) | async-done | bytes 2293776 | tf_op jit(solution)/shard_map/psum | solution.py:79
  83.9 0.0 copy-start.4
  83.9 2.6 %fusion.3 = (f32[160]{0:T(256)S(1)}, f32[160]{0:T(256)S(1)}, f32[160]{0:T(256)S(1)}, bf16[160,3584]{1,0:T(8,128)(2,1)S(1)}) fusion(bf16[160,3584]{1,0:T(8,128)(2,1)} %get-tuple-element.6, bf16[160,3584]{1,0:T(8,128)(2,1)} %get-tuple-element.5, bf16[160,3584]{1,0:T(8,128)(2,1)S(1)} %copy-done.2), kind=kLoop, calls=%fused_computation.11 | loop fusion | flops 6880800 | bytes 4589440 | tf_op jit(solution)/shard_map/reduce_sum | solution.py:87
  86.5 0.0 copy-start.3
  86.5 0.0 copy-done.4
  86.5 0.8 fusion.5
  87.3 0.2 copy-done.3
  87.5 0.0 copy-start.1
  87.5 0.0 copy-start.10
  87.5 0.8 fusion.25
  88.2 0.4 copy-done.10
  88.7 0.2 fusion.30
  88.9 0.0 copy-done.1
  88.9 0.2 convolution_bitcast_fusion
  89.1 2.0 %fusion.31 = bf16[160,1,128]{2,0,1:T(8,128)(2,1)} fusion(f32[2,160,160]{1,2,0:T(8,128)S(1)} %convolution_bitcast_fusion, bf16[20,2,8,128]{3,2,1,0:T(8,128)(2,1)} %fusion.24, f32[2,160,160]{1,2,0:T(8,128)} %get-tuple-element.14, f32[2,160]{1,0:T(2,128)S(1)} %get-tuple-element.13), kind=kOutput, calls=%fused_computation.46 | convolution fusion | flops 13486559 | bytes 533760 | tf_op jit(solution)/shard_map/epk,peh->kh/dot_general | solution.py:106
  91.1 1.4 %fusion.23 = bf16[2,20,8,128]{3,2,1,0:T(8,128)(2,1)S(1)} fusion(f32[2,160,160]{1,2,0:T(8,128)S(1)} %convolution_bitcast_fusion, bf16[160,1,128]{2,1,0:T(2,128)(2,1)S(1)} %get-tuple-element.10, f32[2,160,160]{1,2,0:T(8,128)} %get-tuple-element.14, f32[2,160]{1,0:T(2,128)S(1)} %get-tuple-element.13), kind=kOutput, calls=%fused_computation.38 | convolution fusion | flops 13507039 | bytes 533760 | tf_op jit(solution)/shard_map/epk,kh->peh/dot_general | solution.py:102
  92.5 0.0 copy-start.6
  92.5 0.0 copy-start.8
  92.5 2.4 %fusion.45 = f32[160,3584]{1,0:T(8,128)S(1)} fusion(bf16[3584,256]{1,0:T(8,128)(2,1)} %param.14, bf16[2,20,8,128]{3,2,1,0:T(8,128)(2,1)S(1)} %fusion.23), kind=kOutput, calls=%fused_computation.66 | convolution fusion | flops 293601280 | bytes 4210688 | tf_op jit(solution)/shard_map/dot_general | solution.py:111
  94.9 0.0 copy-done.6
  94.9 0.0 copy-done.8
  94.9 1.8 %fusion.2 = bf16[160,3584]{1,0:T(8,128)(2,1)} fusion(f32[160,3584]{1,0:T(8,128)S(1)} %fusion.45, bf16[3584,256]{1,0:T(8,128)(2,1)S(1)} %copy-done.6, bf16[160,1,128]{2,0,1:T(8,128)(2,1)S(1)} %fusion.30, bf16[160,1,128]{2,0,1:T(8,128)(2,1)S(1)} %copy-done.8), kind=kOutput, calls=%fused_computation.3 | convolution fusion | flops 294789120 | bytes 5357568 | tf_op jit(solution)/shard_map/dot_general | solution.py:117
  96.7 0.0 reduce-scatter.2.cloned.1.call-update
  96.7 1.6 %convert_element_type.73 = f32[160,3584]{1,0:T(8,128)} convert(bf16[160,3584]{1,0:T(8,128)(2,1)S(1)} %copy-done.2) | non-fusion elementwise | flops 573440 | bytes 3440640 | tf_op jit(solution)/shard_map/convert_element_type | solution.py:40
  98.3 0.1 dynamic-slice.3
  98.4 24.2 %reduce-scatter.2.cloned.1.call-done = bf16[40,3584]{1,0:T(8,128)(2,1)} async-done(((bf16[160,3584]{1,0:T(8,128)(2,1)}), bf16[40,3584]{1,0:T(8,128)(2,1)}) %reduce-scatter.2.cloned.1.call-update) | async-done | bytes 286736 | tf_op jit(solution)/shard_map/reduce_scatter | solution.py:114
  122.6 1.3 multiply_reduce_fusion.2
  123.9 2.3 %add_convert_fusion.1 = bf16[40,3584]{1,0:T(8,128)(2,1)} fusion(bf16[40,3584]{1,0:T(8,128)(2,1)} %reduce-scatter.2.cloned.1.call-done, f32[160,3584]{1,0:T(8,128)} %copy-done.1, s32[]{:T(128)S(6)} %select_n.14, f32[160,3584]{1,0:T(8,128)} %convert_element_type.73, f32[40]{0:T(128)S(1)} %broadcast_multiply_fusion, f32[3584]{0:T(1024)S(1)} %copy-done.7, ...), kind=kLoop, calls=%fused_computation.50 | loop fusion | flops 1433600 | bytes 1734980 | tf_op jit(solution)/shard_map/convert_element_type | solution.py:133
  (6 shorter events, 0.1 us)
Async XLA Ops:
  7.2 14.2 %copy-start = (bf16[256,3584]{1,0:T(8,128)(2,1)S(1)}, bf16[256,3584]{1,0:T(8,128)(2,1)}, u32[]{:S(2)}) copy-start(bf16[256,3584]{1,0:T(8,128)(2,1)} %param.16) | copy-start | bytes 5505028
  7.2 76.7 %all-reduce.3.cloned.1.call-start = ((), (), s32[]{:S(2)}) async-start(), calls=%async_computation.2 | async-start | bytes 4587520 | tf_op jit(solution)/shard_map/psum | solution.py:79
  8.2 14.7 %collective-permute-start = (bf16[32,1024]{1,0:T(8,128)(2,1)S(1)}, bf16[32,1024]{1,0:T(8,128)(2,1)}, u32[]{:S(2)}, u32[]{:S(2)}) collective-permute-start(bf16[32,1024]{1,0:T(8,128)(2,1)S(1)} %slice.11), channel_id=1, source_target_pairs={{0,4},{4,8},{8,12},{12,16},{16,20},{20,24},{24,28},{1,5},{5,9},{9,... | collective-permute-start | bytes 196616 | tf_op jit(solution)/shard_map/ppermute | solution.py:18
  12.0 5.5 %copy-start.2 = (bf16[160,3584]{1,0:T(8,128)(2,1)S(1)}, bf16[160,3584]{1,0:T(8,128)(2,1)}, u32[]{:S(2)}) copy-start(bf16[160,3584]{1,0:T(8,128)(2,1)} %param.12) | copy-start | bytes 3440644
  12.0 5.5 %copy-start.5 = (bf16[3584,256]{1,0:T(8,128)(2,1)S(1)}, bf16[3584,256]{1,0:T(8,128)(2,1)}, u32[]{:S(2)}) copy-start(bf16[3584,256]{1,0:T(8,128)(2,1)} %param.15) | copy-start | bytes 5505028
  12.0 5.5 %copy-start.7 = (f32[3584]{0:T(1024)S(1)}, f32[3584]{0:T(1024)}, u32[]{:S(2)}) copy-start(f32[3584]{0:T(1024)} %param.13) | copy-start | bytes 43012
  20.1 2.8 %copy-start.9 = (bf16[128,1024]{1,0:T(8,128)(2,1)S(1)}, bf16[128,1024]{1,0:T(8,128)(2,1)}, u32[]{:S(2)}) copy-start(bf16[128,1024]{1,0:T(8,128)(2,1)} %param.10) | copy-start | bytes 786436
  28.5 94.1 %reduce-scatter.2.cloned.1.call-start = ((), (), s32[]{:S(2)}) async-start(), calls=%async_computation.1 | async-start | bytes 1433600 | tf_op jit(solution)/shard_map/reduce_scatter | solution.py:114
  83.9 2.6 %copy-start.4 = (bf16[160,3584]{1,0:T(8,128)(2,1)S(1)}, bf16[160,3584]{1,0:T(8,128)(2,1)}, u32[]{:S(2)}) copy-start(bf16[160,3584]{1,0:T(8,128)(2,1)} %get-tuple-element.6) | copy-start | bytes 3440644
  86.5 1.0 copy-start.3
  87.5 1.4 %copy-start.1 = (f32[160,3584]{1,0:T(8,128)}, f32[160,3584]{1,0:T(8,128)S(1)}, u32[]{:S(2)}) copy-start(f32[160,3584]{1,0:T(8,128)S(1)} %fusion.5) | copy-start | bytes 6881284
  87.5 1.2 copy-start.10
  92.5 2.4 %copy-start.6 = (bf16[3584,256]{1,0:T(8,128)(2,1)S(1)}, bf16[3584,256]{1,0:T(8,128)(2,1)}, u32[]{:S(2)}) copy-start(bf16[3584,256]{1,0:T(8,128)(2,1)} %param.15) | copy-start | bytes 5505028
  92.5 2.4 %copy-start.8 = (bf16[160,1,128]{2,0,1:T(8,128)(2,1)S(1)}, bf16[160,1,128]{2,0,1:T(8,128)(2,1)}, u32[]{:S(2)}) copy-start(bf16[160,1,128]{2,0,1:T(8,128)(2,1)} %fusion.31) | copy-start | bytes 122884
Sparse Core Ops, SparseCore 0:
  28.6 55.2 all-reduce.2
  96.9 25.6 reduce-scatter.1
where the time goes:
time: 135 us; the launch traced here: 133 us
  waiting for transfers between devices  78.9 us (58%)
  matrix products  22.5 us (17%)
  between operations  15.5 us (11%)
  other arithmetic  11 us (8%)
  starting transfers between devices  3.19 us (2%)
  local copies, waits for them, and re-layouts  1.91 us (1%)
    psum x1, waiting for transfers between devices, body(): lax.psum(branch_part, 'tp').astype(jnp.float32)  54.7 us
    reduce_scatter x1, waiting for transfers between devices, body(): lax.psum_scatter((total + lax.dot_general(d_keyval, w_keyval, (((1,), (1,...  24.2 us
    dot_general x1, matrix products, body(): jnp.dot(picked, proj_weight, preferred_element_type=jnp.float32)  5.57 us
    ppermute x1, starting transfers between devices, from_behind(): return lax.ppermute(block, axis, route)  3.11 us
    dot_general x1, matrix products, body(): jnp.dot(normed, w_query, preferred_element_type=jnp.float32)  3.02 us
  transfers between devices with their start and end apart: 3, of which 2 were waited for; matrix products, arithmetic and copies ran while one was open for 9% of the time, Pallas kernels for 0%

commit v1 on v0

--- a/solution.py
+++ b/solution.py
@@ -1,8 +1,11 @@
+import functools
 import math
 
 import jax
 import jax.numpy as jnp
 from jax import lax
+from jax.experimental import pallas as pl
+from jax.experimental.pallas import tpu as pltpu
 from jax.sharding import PartitionSpec as P
 
 HD = 128
@@ -18,7 +21,7 @@
     return lax.ppermute(block, axis, route)
 
 
-def body(
+def plain_body(
     teacher_hidden,
     proj_weight,
     student_in,
@@ -134,6 +137,498 @@
     return (student_out, grad_in)
 
 
+MESH = pl.DeviceIdType.MESH
+NT = (((1,), (1,)), ((), ()))
+TN = (((0,), (0,)), ((), ()))
+F32 = jnp.float32
+BF16 = jnp.bfloat16
+
+
+def dot(a, b, dims=None):
+    if dims is None:
+        return jnp.dot(a, b, preferred_element_type=F32)
+    return lax.dot_general(a, b, dims, preferred_element_type=F32)
+
+
+def step_kernel(
+    n_seq,
+    offset_ref,
+    count_ref,
+    start_ref,
+    gain_ref,
+    teacher_hbm,
+    proj_hbm,
+    x_hbm,
+    wq_hbm,
+    wkv_hbm,
+    wo_hbm,
+    out_ref,
+    grad_ref,
+    feat,
+    proj,
+    x_in,
+    wq,
+    wkv,
+    wo,
+    xq,
+    normed,
+    inv_s,
+    qkv,
+    probs_s,
+    attn_s,
+    g_part,
+    g_near,
+    g_chip,
+    g_far,
+    b_part,
+    b_near,
+    b_chip,
+    b_far,
+    t_s,
+    y_s,
+    dy_s,
+    dy_own,
+    d_attn_s,
+    dd_s,
+    n_part,
+    n_near,
+    n_chip,
+    n_far,
+    dn_s,
+    load_sem,
+    proj_sem,
+    send_sem,
+    recv_sem,
+    shift_sem,
+):
+    rows, width = x_in.shape
+    quarter = rows // 4
+    chunks, _, chunk = proj.shape
+    own_tokens = teacher_hbm.shape[0]
+    shift = rows - own_tokens
+    s = lax.axis_index("seq")
+    me = lax.axis_index("tp")
+    c = lax.rem(me, 2)
+    y = me // 2
+    near = {"tp": y * 2 + 1 - c}
+    far = {"tp": (1 - y) * 2 + c}
+    scale = 1.0 / math.sqrt(HD)
+
+    def cols(k):
+        return pl.ds(pl.multiple_of(k * chunk, chunk), chunk)
+
+    loads = [
+        pltpu.make_async_copy(a, b, load_sem.at[i])
+        for i, (a, b) in enumerate(
+            [
+                (x_hbm, x_in),
+                (wq_hbm, wq),
+                (wkv_hbm, wkv),
+                (teacher_hbm, feat.at[pl.ds(shift, own_tokens)]),
+                (wo_hbm, wo),
+            ]
+        )
+    ]
+    for one in loads[:4]:
+        one.start()
+
+    def proj_load(k):
+        return pltpu.make_async_copy(proj_hbm.at[:, cols(k)], proj.at[k], proj_sem.at[k])
+
+    def start_proj(k, _):
+        proj_load(k).start()
+        return 0
+
+    lax.fori_loop(0, chunks, start_proj, 0)
+    loads[4].start()
+
+    barrier = pltpu.get_barrier_semaphore()
+    pl.semaphore_signal(barrier, inc=1, device_id=near, device_id_type=MESH)
+    pl.semaphore_signal(barrier, inc=1, device_id=far, device_id_type=MESH)
+
+    @pl.when(s > 0)
+    def _():
+        pl.semaphore_signal(barrier, inc=1, device_id={"seq": s - 1}, device_id_type=MESH)
+
+    @pl.when(s < n_seq - 1)
+    def _():
+        pl.semaphore_signal(barrier, inc=1, device_id={"seq": s + 1}, device_id_type=MESH)
+
+    inner = (s > 0) & (s < n_seq - 1)
+
+    @pl.when(inner)
+    def _():
+        pl.semaphore_wait(barrier, 4)
+
+    @pl.when(jnp.logical_not(inner))
+    def _():
+        pl.semaphore_wait(barrier, 3)
+
+    def shift_copy(to):
+        return pltpu.make_async_remote_copy(
+            src_ref=teacher_hbm.at[pl.ds(own_tokens - shift, shift)],
+            dst_ref=feat.at[pl.ds(0, shift)],
+            send_sem=shift_sem.at[0],
+            recv_sem=shift_sem.at[1],
+            device_id={"seq": to},
+            device_id_type=MESH,
+        )
+
+    @pl.when(s < n_seq - 1)
+    def _():
+        shift_copy(s + 1).start()
+
+    @pl.when(s == 0)
+    def _():
+        feat[0:shift, :] = jnp.zeros((shift, feat.shape[1]), BF16)
+
+    def remote(kind, k, src, dst, to):
+        return pltpu.make_async_remote_copy(
+            src_ref=src,
+            dst_ref=dst,
+            send_sem=send_sem.at[kind, k],
+            recv_sem=recv_sem.at[kind, k],
+            device_id=to,
+            device_id_type=MESH,
+        )
+
+    def split_store(ref, k, val):
+        for q in range(4):
+            ref[k, q % 2, q // 2] = val[q * quarter : (q + 1) * quarter].astype(BF16)
+
+    loads[0].wait()
+
+    def square(k, acc):
+        v = x_in[:, cols(k)].astype(F32)
+        for q in range(4):
+            xq[q % 2, q // 2, :, cols(k)] = v[q * quarter : (q + 1) * quarter]
+        return acc + jnp.sum(v * v, axis=1, keepdims=True)
+
+    total = lax.fori_loop(0, chunks, square, jnp.zeros((rows, 1), F32))
+    inv = lax.rsqrt(total / width + epsilon)
+    for q in range(4):
+        inv_s[q] = inv[q * quarter : (q + 1) * quarter]
+
+    def norm(k, _):
+        v = x_in[:, cols(k)].astype(F32)
+        normed[:, cols(k)] = (v * inv * gain_ref[:, cols(k)]).astype(BF16)
+        return 0
+
+    lax.fori_loop(0, chunks, norm, 0)
+
+    start = offset_ref[0] - s * own_tokens + shift
+    r_i = lax.broadcasted_iota(jnp.int32, (rows, rows), 0)
+    c_i = lax.broadcasted_iota(jnp.int32, (rows, rows), 1)
+
+    @pl.when(s > 0)
+    def _():
+        shift_copy(s).wait_recv()
+
+    loads[3].wait()
+    select = jnp.where(c_i == r_i + start, 1.0, 0.0).astype(BF16)
+    feat[...] = dot(select, feat[...]).astype(BF16)
+
+    def near_copy(kind, k, part, land):
+        return remote(kind, k, part.at[k, 1 - c], land.at[k], near)
+
+    def far_copy(kind, k, chip, land):
+        return remote(kind, k, chip.at[k], land.at[k], far)
+
+    def pass_on(kind, k, part, land, chip, far_land):
+        near_copy(kind, k, part, land).wait_recv()
+        chip[k] = (part[k, c].astype(F32) + land[k].astype(F32)).astype(BF16)
+        far_copy(kind + 1, k, chip, far_land).start()
+
+    def goal_step(k, _):
+        proj_load(k).wait()
+        split_store(g_part, k, dot(feat[...], proj[k]))
+        near_copy(0, k, g_part, g_near).start()
+
+        @pl.when(k > 0)
+        def _():
+            pass_on(0, k - 1, g_part, g_near, g_chip, g_far)
+
+        return 0
+
+    lax.fori_loop(0, chunks, goal_step, 0)
+
+    loads[1].wait()
+    loads[2].wait()
+    qkv[:, 0 : QPK * HD] = dot(normed[...], wq[...]).astype(BF16)
+    pass_on(0, chunks - 1, g_part, g_near, g_chip, g_far)
+    qkv[:, QPK * HD :] = dot(normed[...], wkv[...]).astype(BF16)
+
+    starts = jnp.sum(
+        jnp.where(r_i == c_i, start_ref[...].astype(F32), 0.0), axis=1, keepdims=True
+    )
+    c_f = c_i.astype(F32)
+    allowed = (c_f >= starts) & (c_i <= r_i)
+    keys = qkv[:, QPK * HD : (QPK + 1) * HD]
+    values = qkv[:, (QPK + 1) * HD :]
+    for e in range(QPK):
+        scores = dot(qkv[:, e * HD : (e + 1) * HD], keys, NT) * scale
+        scores = jnp.where(allowed, scores, -jnp.inf)
+        expo = jnp.exp(scores - jnp.max(scores, axis=-1, keepdims=True))
+        probs = expo / jnp.sum(expo, axis=-1, keepdims=True)
+        probs_s[e] = probs
+        attn_s[:, e * HD : (e + 1) * HD] = dot(probs.astype(BF16), values).astype(BF16)
+
+    loads[4].wait()
+
+    def branch_step(k, _):
+        split_store(b_part, k, dot(attn_s[...], wo[:, cols(k)]))
+        near_copy(2, k, b_part, b_near).start()
+
+        @pl.when(k > 0)
+        def _():
+            pass_on(2, k - 1, b_part, b_near, b_chip, b_far)
+
+        return 0
+
+    lax.fori_loop(0, chunks, branch_step, 0)
+    pass_on(2, chunks - 1, b_part, b_near, b_chip, b_far)
+
+    def y_copy(k):
+        return remote(4, k, y_s.at[k, c], y_s.at[k, c], near)
+
+    def loss_step(k, sums):
+        asum, bsum, both = sums
+        far_copy(1, k, g_chip, g_far).wait_recv()
+        far_copy(3, k, b_chip, b_far).wait_recv()
+        t = (g_chip[k].astype(F32) + g_far[k].astype(F32)).astype(BF16).astype(F32)
+        t_s[k] = t
+        branch = b_chip[k].astype(F32) + b_far[k].astype(F32)
+        out = (xq[c, :, :, cols(k)] + branch).astype(BF16)
+        y_s[k, c] = out
+        y_copy(k).start()
+        out = out.astype(F32)
+        return (
+            asum + jnp.sum(out * out, axis=-1, keepdims=True),
+            bsum + jnp.sum(t * t, axis=-1, keepdims=True),
+            both + jnp.sum(out * t, axis=-1, keepdims=True),
+        )
+
+    zero = jnp.zeros((2, quarter, 1), F32)
+    asum, bsum, both_sum = lax.fori_loop(0, chunks, loss_step, (zero, zero, zero))
+    asum = asum + epsilon
+    bsum = bsum + epsilon
+    both = lax.rsqrt(asum * bsum)
+    cosv = both_sum * both
+    slot = (
+        lax.broadcasted_iota(jnp.int32, (2, quarter, 1), 0) * (2 * quarter)
+        + lax.broadcasted_iota(jnp.int32, (2, quarter, 1), 1)
+        + c * quarter
+    )
+    live = jnp.where(slot < count_ref[0], -math.sqrt(width), 0.0)
+    t_factor = live * both
+    y_factor = live * cosv / asum
+
+    def dy_copy(k):
+        return remote(5, k, dy_s.at[k, c], dy_s.at[k, c], near)
+
+    def dy_step(k, _):
+        dy = t_s[k] * t_factor - y_s[k, c].astype(F32) * y_factor
+        dy_s[k, c] = dy.astype(BF16)
+        dy_copy(k).start()
+        dy_own[:, :, cols(k)] = dy
+        return 0
+
+    lax.fori_loop(0, chunks, dy_step, 0)
+
+    d_attn_s[...] = jnp.zeros_like(d_attn_s)
+
+    def d_attn_step(k, _):
+        dy_copy(k).wait_recv()
+        dy = jnp.concatenate(
+            [dy_s[k, q % 2, q // 2].astype(F32) for q in range(4)], axis=0
+        ).astype(BF16)
+        d_attn_s[...] += dot(dy, wo[:, cols(k)], NT)
+        return 0
+
+    lax.fori_loop(0, chunks, d_attn_step, 0)
+
+    d_values = jnp.zeros((rows, HD), F32)
+    d_keys = jnp.zeros((rows, HD), F32)
+    for e in range(QPK):
+        probs = probs_s[e]
+        d_out = d_attn_s[:, e * HD : (e + 1) * HD].astype(BF16)
+        d_values += dot(probs.astype(BF16), d_out, TN)
+        dprob = dot(d_out, values, NT)
+        dscore = probs * (dprob - jnp.sum(dprob * probs, axis=-1, keepdims=True)) * scale
+        dscore_b = dscore.astype(BF16)
+        dd_s[:, e * HD : (e + 1) * HD] = dot(dscore_b, keys).astype(BF16)
+        d_keys += dot(dscore_b, qkv[:, e * HD : (e + 1) * HD], TN)
+    dd_s[:, QPK * HD : (QPK + 1) * HD] = d_keys.astype(BF16)
+    dd_s[:, (QPK + 1) * HD :] = d_values.astype(BF16)
+
+    def n_pass_on(k):
+        near_copy(6, k, n_part, n_near).wait_recv()
+        both_parts = n_part[k, c, 1 - y].astype(F32) + n_near[k, 1 - y].astype(F32)
+        n_chip[k] = both_parts.astype(BF16)
+        far_copy(7, k, n_chip, n_far).start()
+
+    def n_step(k, _):
+        val = dot(dd_s[:, 0 : QPK * HD], wq[cols(k), :], NT) + dot(
+            dd_s[:, QPK * HD :], wkv[cols(k), :], NT
+        )
+        split_store(n_part, k, val)
+        near_copy(6, k, n_part, n_near).start()
+
+        @pl.when(k > 0)
+        def _():
+            n_pass_on(k - 1)
+
+        return 0
+
+    lax.fori_loop(0, chunks, n_step, 0)
+    n_pass_on(chunks - 1)
+
+    def out_step(k, _):
+        y_copy(k).wait_recv()
+        for q in range(4):
+            out_ref[q, :, cols(k)] = y_s[k, q % 2, q // 2]
+        return 0
+
+    lax.fori_loop(0, chunks, out_step, 0)
+
+    def sum_step(k, acc):
+        far_copy(7, k, n_chip, n_far).wait_recv()
+        val = n_part[k, c, y].astype(F32) + n_near[k, y].astype(F32) + n_far[k].astype(F32)
+        upper = val * gain_ref[:, cols(k)]
+        dn_s[:, cols(k)] = upper
+        return acc + jnp.sum(upper * xq[c, y, :, cols(k)], axis=-1, keepdims=True)
+
+    acc = lax.fori_loop(0, chunks, sum_step, jnp.zeros((quarter, 1), F32))
+    inv_own = inv_s[y * 2 + c]
+    x_factor = inv_own * inv_own * inv_own * (acc / width)
+
+    def grad_step(k, _):
+        dx = inv_own * dn_s[:, cols(k)] - xq[c, y, :, cols(k)] * x_factor
+        grad_ref[:, cols(k)] = (dy_own[y, :, cols(k)] + dx).astype(BF16)
+        return 0
+
+    lax.fori_loop(0, chunks, grad_step, 0)
+
+    def drain(k, _):
+        near_copy(0, k, g_part, g_near).wait_send()
+        far_copy(1, k, g_chip, g_far).wait_send()
+        near_copy(2, k, b_part, b_near).wait_send()
+        far_copy(3, k, b_chip, b_far).wait_send()
+        y_copy(k).wait_send()
+        dy_copy(k).wait_send()
+        near_copy(6, k, n_part, n_near).wait_send()
+        far_copy(7, k, n_chip, n_far).wait_send()
+        return 0
+
+    lax.fori_loop(0, chunks, drain, 0)
+
+    @pl.when(s < n_seq - 1)
+    def _():
+        shift_copy(s + 1).wait_send()
+
+
+def chunk_of(width):
+    for size in (512, 256, 128):
+        if width % size == 0:
+            return size
+    return width
+
+
+def fused_body(
+    teacher_hidden,
+    proj_weight,
+    student_in,
+    norm_gain,
+    w_query,
+    w_keyval,
+    w_out,
+    row_offsets,
+    row_counts,
+    doc_start,
+):
+    rows, width = student_in.shape
+    depth = teacher_hidden.shape[1]
+    heads = w_query.shape[1]
+    quarter = rows // 4
+    chunk = chunk_of(width)
+    k = width // chunk
+    vmem = pltpu.VMEM
+    half = (k, 2, quarter, chunk)
+    parts = (k, 2, 2, quarter, chunk)
+    scratch = [
+        vmem((rows, depth), BF16),
+        vmem((k, depth, chunk), BF16),
+        vmem((rows, width), BF16),
+        vmem(w_query.shape, BF16),
+        vmem(w_keyval.shape, BF16),
+        vmem(w_out.shape, BF16),
+        vmem((2, 2, quarter, width), F32),
+        vmem((rows, width), BF16),
+        vmem((4, quarter, 1), F32),
+        vmem((rows, 2 * heads), BF16),
+        vmem((QPK, rows, rows), F32),
+        vmem((rows, heads), BF16),
+        vmem(parts, BF16),
+        vmem(half, BF16),
+        vmem(half, BF16),
+        vmem(half, BF16),
+        vmem(parts, BF16),
+        vmem(half, BF16),
+        vmem(half, BF16),
+        vmem(half, BF16),
+        vmem(half, F32),
+        vmem(parts, BF16),
+        vmem(parts, BF16),
+        vmem((2, quarter, width), F32),
+        vmem((rows, heads), F32),
+        vmem((rows, 2 * heads), BF16),
+        vmem(parts, BF16),
+        vmem(half, BF16),
+        vmem((k, quarter, chunk), BF16),
+        vmem((k, quarter, chunk), BF16),
+        vmem((quarter, width), F32),
+        pltpu.SemaphoreType.DMA((5,)),
+        pltpu.SemaphoreType.DMA((k,)),
+        pltpu.SemaphoreType.DMA((8, k)),
+        pltpu.SemaphoreType.DMA((8, k)),
+        pltpu.SemaphoreType.DMA((2,)),
+    ]
+    smem = pl.BlockSpec(memory_space=pltpu.SMEM)
+    in_vmem = pl.BlockSpec(memory_space=pltpu.VMEM)
+    anywhere = pl.BlockSpec(memory_space=pl.ANY)
+    flops = 2 * rows * width * (depth + 6 * heads)
+    moved = 2 * width * (depth + 3 * heads + 3 * rows)
+    student_out, grad_in = pl.pallas_call(
+        functools.partial(step_kernel, lax.axis_size("seq")),
+        out_shape=(
+            jax.ShapeDtypeStruct((4, quarter, width), BF16),
+            jax.ShapeDtypeStruct((quarter, width), BF16),
+        ),
+        in_specs=[smem, smem, in_vmem, in_vmem] + [anywhere] * 6,
+        out_specs=(in_vmem, in_vmem),
+        scratch_shapes=scratch,
+        cost_estimate=pl.CostEstimate(flops=flops, bytes_accessed=moved, transcendentals=0),
+        compiler_params=pltpu.CompilerParams(
+            collective_id=0, has_side_effects=True, vmem_limit_bytes=VMEM_BYTES
+        ),
+    )(
+        row_offsets,
+        row_counts,
+        doc_start.reshape(1, rows),
+        norm_gain.reshape(1, width),
+        teacher_hidden,
+        proj_weight,
+        student_in,
+        w_query,
+        w_keyval,
+        w_out,
+    )
+    return (student_out.reshape(rows, width), grad_in)
+
+
+VMEM_BYTES = 52 * 2**20
+
+
 def solution(mesh):
     in_specs = (
         P("seq", "tp"),
@@ -148,4 +643,5 @@
         P("seq"),
     )
     out_specs = (P("seq", None), P(("seq", "tp"), None))
+    body = fused_body if mesh.shape["tp"] == 4 else plain_body
     return jax.shard_map(body, mesh=mesh, in_specs=in_specs, out_specs=out_specs, check_vma=False)

time: 135 us -> 54.3 us (0.40); the launches traced: 133 us -> 54 us
  waiting for transfers between devices: 78.9 us -> 0 us
  Pallas kernels: 0 us -> 48 us
  matrix products: 22.5 us -> 0 us
  between operations: 15.5 us -> 1.94 us
  other arithmetic: 11 us -> 0 us
  starting transfers between devices: 3.19 us -> 0 us
  local copies, waits for them, and re-layouts: 1.91 us -> 4.07 us
    psum x1 -> x0, waiting for transfers between devices: 54.7 us -> none  [body(): lax.psum(branch_part, 'tp').astype(jnp.float32)]
    pallas_call x0 -> x1, Pallas kernels: none -> 48 us  [fused_body(): pl.pallas_call(functools.partial(step_kernel, lax.axis_size('seq')), out_...]
    reduce_scatter x1 -> x0, waiting for transfers between devices: 24.2 us -> none  [body(): lax.psum_scatter((total + lax.dot_general(d_keyval, w_keyval, (((1,), (1,...]
    dot_general x12 -> x0, matrix products: 20.6 us -> none  [the longest x1 5.57 us: body(): jnp.dot(picked, proj_weight, preferred_element_type=jnp.float32)]
    reduce_sum x3 -> x0, other arithmetic: 5.62 us -> none  [the longest x1 2.57 us: body(): bsum = jnp.sum(tf * tf, axis=1, keepdims=True) + epsilon]
    convert_element_type x2 -> x0, other arithmetic: 3.86 us -> none  [the longest x1 2.26 us: body(): grad_in = (dy_own + dx).astype(jnp.bfloat16)]
    ppermute x1 -> x0, starting transfers between devices: 3.11 us -> none  [from_behind(): return lax.ppermute(block, axis, route)]
    unnamed x22 -> x6, local copies, waits for them, and re-layouts: 0.64 us -> 3.34 us
  transfers between devices with their start and end apart: 3 -> 0, of which waited for: 2 -> 0; matrix products, arithmetic and copies ran while one was open for 9% -> 0% of each run, Pallas kernels for 0% -> 0%
where the time goes in v1:
time: 54.3 us; the launch traced here: 54 us
  Pallas kernels  48 us (88%)
  local copies, waits for them, and re-layouts  4.07 us (7%)
  between operations  1.94 us (4%)
    pallas_call x1, Pallas kernels, fused_body(): pl.pallas_call(functools.partial(step_kernel, lax.axis_size('seq')), out_...  48 us
    unnamed x6, local copies, waits for them, and re-layouts  3.34 us

profile of v1, /device:TPU:9, one launch (start us, length us, event | category | flops | bytes accessed | tf_op | source)
XLA Modules:
  0.0 54.0 jit_solution(10261861558106839047)
XLA Ops:
  1.9 0.7 %reshape.14.gain_ref = f32[1,3584]{1,0:T(1,128)S(1)} reshape(f32[3584]{0:T(1024)} %param.13) | data formatting | bytes 28672 | tf_op jit(solution)/shard_map/reshape | solution.py:618
  2.7 0.0 copy-start
  2.7 0.9 %copy-done = bf16[128,1024]{1,0:T(8,128)(2,1)S(1)} copy-done((bf16[128,1024]{1,0:T(8,128)(2,1)S(1)}, bf16[128,1024]{1,0:T(8,128)(2,1)}, u32[]{:S(2)}) %copy-start) | copy-done | bytes 262168
  3.6 0.0 copy-start.1
  3.6 0.7 %copy-done.1 = s32[160]{0:T(256)S(1)} copy-done((s32[160]{0:T(256)S(1)}, s32[160]{0:T(256)}, u32[]{:S(2)}) %copy-start.1) | copy-done | bytes 664
  4.3 48.0 %shard_map.113 = (bf16[4,40,3584]{2,1,0:T(8,128)(2,1)S(1)}, bf16[40,3584]{1,0:T(8,128)(2,1)S(1)}) custom-call(s32[1]{0:T(128)S(6)} %copy.14.offset_ref, s32[1]{0:T(128)S(6)} %copy.15.count_ref, s32[1,160]{1,0:T(1,128)S(1)} %bitcast.3, f32[1,3584]{1,0:T(1,128)S(1)} %reshape.14.gain_ref, bf16[128,1024]{1,0:T(8,128)(2,1)S(1)} %copy-done, ...), custom_call_target="tpu_custom_call" | custom-call | flops 2936012800 | bytes 16285696 | tf_op jit(solution)/shard_map/pallas_call | solution.py:601
  52.3 1.0 %copy.16 = bf16[160,3584]{1,0:T(8,128)(2,1)} copy(bf16[160,3584]{1,0:T(8,128)(2,1)S(1)} %bitcast.2) | data formatting | bytes 2293760
  53.3 0.7 %copy.17 = bf16[40,3584]{1,0:T(8,128)(2,1)} copy(bf16[40,3584]{1,0:T(8,128)(2,1)S(1)} %get-tuple-element.9) | data formatting | bytes 573440
Async XLA Ops:
  2.7 1.0 %copy-start = (bf16[128,1024]{1,0:T(8,128)(2,1)S(1)}, bf16[128,1024]{1,0:T(8,128)(2,1)}, u32[]{:S(2)}) copy-start(bf16[128,1024]{1,0:T(8,128)(2,1)} %teacher_hbm.1) | copy-start | bytes 786436
  3.6 0.7 %copy-start.1 = (s32[160]{0:T(256)S(1)}, s32[160]{0:T(256)}, u32[]{:S(2)}) copy-start(s32[160]{0:T(256)} %param.19) | copy-start | bytes 1924

commit v2 on v1

--- a/solution.py
+++ b/solution.py
@@ -154,8 +154,8 @@
     n_seq,
     offset_ref,
     count_ref,
-    start_ref,
-    gain_ref,
+    start_hbm,
+    gain_hbm,
     teacher_hbm,
     proj_hbm,
     x_hbm,
@@ -164,6 +164,8 @@
     wo_hbm,
     out_ref,
     grad_ref,
+    start_s,
+    gain_s,
     feat,
     proj,
     x_in,
@@ -200,6 +202,7 @@
     send_sem,
     recv_sem,
     shift_sem,
+    out_sem,
 ):
     rows, width = x_in.shape
     quarter = rows // 4
@@ -214,6 +217,9 @@
     far = {"tp": (1 - y) * 2 + c}
     scale = 1.0 / math.sqrt(HD)
 
+    def gain(k):
+        return gain_s[cols(k)][None, :]
+
     def cols(k):
         return pl.ds(pl.multiple_of(k * chunk, chunk), chunk)
 
@@ -226,11 +232,13 @@
                 (wkv_hbm, wkv),
                 (teacher_hbm, feat.at[pl.ds(shift, own_tokens)]),
                 (wo_hbm, wo),
+                (start_hbm, start_s),
+                (gain_hbm, gain_s),
             ]
         )
     ]
-    for one in loads[:4]:
-        one.start()
+    loads[3].start()
+    loads[0].start()
 
     def proj_load(k):
         return pltpu.make_async_copy(proj_hbm.at[:, cols(k)], proj.at[k], proj_sem.at[k])
@@ -240,7 +248,8 @@
         return 0
 
     lax.fori_loop(0, chunks, start_proj, 0)
-    loads[4].start()
+    for i in (1, 2, 6, 5, 4):
+        loads[i].start()
 
     barrier = pltpu.get_barrier_semaphore()
     pl.semaphore_signal(barrier, inc=1, device_id=near, device_id_type=MESH)
@@ -309,13 +318,6 @@
     for q in range(4):
         inv_s[q] = inv[q * quarter : (q + 1) * quarter]
 
-    def norm(k, _):
-        v = x_in[:, cols(k)].astype(F32)
-        normed[:, cols(k)] = (v * inv * gain_ref[:, cols(k)]).astype(BF16)
-        return 0
-
-    lax.fori_loop(0, chunks, norm, 0)
-
     start = offset_ref[0] - s * own_tokens + shift
     r_i = lax.broadcasted_iota(jnp.int32, (rows, rows), 0)
     c_i = lax.broadcasted_iota(jnp.int32, (rows, rows), 1)
@@ -336,30 +338,59 @@
 
     def pass_on(kind, k, part, land, chip, far_land):
         near_copy(kind, k, part, land).wait_recv()
-        chip[k] = (part[k, c].astype(F32) + land[k].astype(F32)).astype(BF16)
+        pair = part[k, c, 1 - y].astype(F32) + land[k, 1 - y].astype(F32)
+        chip[k] = pair.astype(BF16)
         far_copy(kind + 1, k, chip, far_land).start()
 
-    def goal_step(k, _):
+    def own_sum(kind, k, part, land, chip, far_land):
+        far_copy(kind + 1, k, chip, far_land).wait_recv()
+        return (
+            part[k, c, y].astype(F32) + land[k, y].astype(F32) + far_land[k].astype(F32)
+        )
+
+    lag = min(2, chunks)
+
+    def scatter(kind, make, part, land, chip, far_land):
+        def step(k, _):
+            split_store(part, k, make(k))
+            near_copy(kind, k, part, land).start()
+
+            @pl.when(k >= lag)
+            def _():
+                pass_on(kind, k - lag, part, land, chip, far_land)
+
+            return 0
+
+        lax.fori_loop(0, chunks, step, 0)
+
+    def scatter_rest(kind, part, land, chip, far_land):
+        for k in range(chunks - lag, chunks):
+            pass_on(kind, k, part, land, chip, far_land)
+
+    def project(k):
         proj_load(k).wait()
-        split_store(g_part, k, dot(feat[...], proj[k]))
-        near_copy(0, k, g_part, g_near).start()
-
-        @pl.when(k > 0)
-        def _():
-            pass_on(0, k - 1, g_part, g_near, g_chip, g_far)
-
-        return 0
-
-    lax.fori_loop(0, chunks, goal_step, 0)
+        return dot(feat[...], proj[k])
+
+    goal_bufs = (g_part, g_near, g_chip, g_far)
+    scatter(0, project, *goal_bufs)
+    loads[6].wait()
+
+    def norm(k, _):
+        v = x_in[:, cols(k)].astype(F32)
+        normed[:, cols(k)] = (v * inv * gain(k)).astype(BF16)
+        return 0
+
+    lax.fori_loop(0, chunks, norm, 0)
 
     loads[1].wait()
     loads[2].wait()
     qkv[:, 0 : QPK * HD] = dot(normed[...], wq[...]).astype(BF16)
-    pass_on(0, chunks - 1, g_part, g_near, g_chip, g_far)
+    scatter_rest(0, *goal_bufs)
     qkv[:, QPK * HD :] = dot(normed[...], wkv[...]).astype(BF16)
+    loads[5].wait()
 
     starts = jnp.sum(
-        jnp.where(r_i == c_i, start_ref[...].astype(F32), 0.0), axis=1, keepdims=True
+        jnp.where(r_i == c_i, start_s[...][None, :].astype(F32), 0.0), axis=1, keepdims=True
     )
     c_f = c_i.astype(F32)
     allowed = (c_f >= starts) & (c_i <= r_i)
@@ -375,32 +406,23 @@
 
     loads[4].wait()
 
-    def branch_step(k, _):
-        split_store(b_part, k, dot(attn_s[...], wo[:, cols(k)]))
-        near_copy(2, k, b_part, b_near).start()
-
-        @pl.when(k > 0)
-        def _():
-            pass_on(2, k - 1, b_part, b_near, b_chip, b_far)
-
-        return 0
-
-    lax.fori_loop(0, chunks, branch_step, 0)
-    pass_on(2, chunks - 1, b_part, b_near, b_chip, b_far)
-
-    def y_copy(k):
-        return remote(4, k, y_s.at[k, c], y_s.at[k, c], near)
+    branch_bufs = (b_part, b_near, b_chip, b_far)
+    scatter(2, lambda k: dot(attn_s[...], wo[:, cols(k)]), *branch_bufs)
+    scatter_rest(2, *branch_bufs)
+
+    def y_copy(kind, k, owner, to):
+        return remote(kind, k, y_s.at[k, c, owner], y_s.at[k, c, owner], to)
+
+    def dy_copy(kind, k, owner, to):
+        return remote(kind, k, dy_s.at[k, c, owner], dy_s.at[k, c, owner], to)
 
     def loss_step(k, sums):
         asum, bsum, both = sums
-        far_copy(1, k, g_chip, g_far).wait_recv()
-        far_copy(3, k, b_chip, b_far).wait_recv()
-        t = (g_chip[k].astype(F32) + g_far[k].astype(F32)).astype(BF16).astype(F32)
+        t = own_sum(0, k, *goal_bufs).astype(BF16).astype(F32)
         t_s[k] = t
-        branch = b_chip[k].astype(F32) + b_far[k].astype(F32)
-        out = (xq[c, :, :, cols(k)] + branch).astype(BF16)
-        y_s[k, c] = out
-        y_copy(k).start()
+        out = (xq[c, y, :, cols(k)] + own_sum(2, k, *branch_bufs)).astype(BF16)
+        y_s[k, c, y] = out
+        y_copy(5, k, y, near).start()
         out = out.astype(F32)
         return (
             asum + jnp.sum(out * out, axis=-1, keepdims=True),
@@ -408,44 +430,57 @@
             both + jnp.sum(out * t, axis=-1, keepdims=True),
         )
 
-    zero = jnp.zeros((2, quarter, 1), F32)
+    zero = jnp.zeros((quarter, 1), F32)
     asum, bsum, both_sum = lax.fori_loop(0, chunks, loss_step, (zero, zero, zero))
+    early = min(2, chunks)
+
+    def start_y(k, _):
+        y_copy(4, k, y, far).start()
+        return 0
+
+    lax.fori_loop(0, early, start_y, 0)
     asum = asum + epsilon
     bsum = bsum + epsilon
     both = lax.rsqrt(asum * bsum)
     cosv = both_sum * both
-    slot = (
-        lax.broadcasted_iota(jnp.int32, (2, quarter, 1), 0) * (2 * quarter)
-        + lax.broadcasted_iota(jnp.int32, (2, quarter, 1), 1)
-        + c * quarter
-    )
+    slot = lax.broadcasted_iota(jnp.int32, (quarter, 1), 0) + (2 * y + c) * quarter
     live = jnp.where(slot < count_ref[0], -math.sqrt(width), 0.0)
     t_factor = live * both
     y_factor = live * cosv / asum
 
-    def dy_copy(k):
-        return remote(5, k, dy_s.at[k, c], dy_s.at[k, c], near)
-
     def dy_step(k, _):
-        dy = t_s[k] * t_factor - y_s[k, c].astype(F32) * y_factor
-        dy_s[k, c] = dy.astype(BF16)
-        dy_copy(k).start()
-        dy_own[:, :, cols(k)] = dy
+        dy = t_s[k] * t_factor - y_s[k, c, y].astype(F32) * y_factor
+        dy_s[k, c, y] = dy.astype(BF16)
+        dy_copy(7, k, y, far).start()
+        dy_copy(8, k, y, near).start()
+        dy_own[:, cols(k)] = dy
         return 0
 
     lax.fori_loop(0, chunks, dy_step, 0)
 
     d_attn_s[...] = jnp.zeros_like(d_attn_s)
 
-    def d_attn_step(k, _):
-        dy_copy(k).wait_recv()
+    def d_attn_part(k):
+        dy_copy(8, k, y, near).wait_recv()
+        dy_copy(9, k, 1 - y, near).wait_recv()
         dy = jnp.concatenate(
             [dy_s[k, q % 2, q // 2].astype(F32) for q in range(4)], axis=0
         ).astype(BF16)
         d_attn_s[...] += dot(dy, wo[:, cols(k)], NT)
+
+    def d_attn_step(k, _):
+        dy_copy(7, k, y, far).wait_recv()
+        dy_copy(9, k, 1 - y, near).start()
+
+        @pl.when(k > 0)
+        def _():
+            d_attn_part(k - 1)
+
         return 0
 
     lax.fori_loop(0, chunks, d_attn_step, 0)
+    lax.fori_loop(early, chunks, start_y, 0)
+    d_attn_part(chunks - 1)
 
     d_values = jnp.zeros((rows, HD), F32)
     d_keys = jnp.zeros((rows, HD), F32)
@@ -461,63 +496,62 @@
     dd_s[:, QPK * HD : (QPK + 1) * HD] = d_keys.astype(BF16)
     dd_s[:, (QPK + 1) * HD :] = d_values.astype(BF16)
 
-    def n_pass_on(k):
-        near_copy(6, k, n_part, n_near).wait_recv()
-        both_parts = n_part[k, c, 1 - y].astype(F32) + n_near[k, 1 - y].astype(F32)
-        n_chip[k] = both_parts.astype(BF16)
-        far_copy(7, k, n_chip, n_far).start()
-
-    def n_step(k, _):
-        val = dot(dd_s[:, 0 : QPK * HD], wq[cols(k), :], NT) + dot(
+    def d_normed(k):
+        return dot(dd_s[:, 0 : QPK * HD], wq[cols(k), :], NT) + dot(
             dd_s[:, QPK * HD :], wkv[cols(k), :], NT
         )
-        split_store(n_part, k, val)
-        near_copy(6, k, n_part, n_near).start()
-
-        @pl.when(k > 0)
-        def _():
-            n_pass_on(k - 1)
-
-        return 0
-
-    lax.fori_loop(0, chunks, n_step, 0)
-    n_pass_on(chunks - 1)
+
+    n_bufs = (n_part, n_near, n_chip, n_far)
+    scatter(10, d_normed, *n_bufs)
+    scatter_rest(10, *n_bufs)
+
+    def forward_y(k, _):
+        y_copy(4, k, y, far).wait_recv()
+        y_copy(6, k, 1 - y, near).start()
+        return 0
+
+    lax.fori_loop(0, chunks, forward_y, 0)
+
+    def out_copy(k, q):
+        return pltpu.make_async_copy(
+            y_s.at[k, q % 2, q // 2], out_ref.at[q, :, cols(k)], out_sem.at[k, q]
+        )
 
     def out_step(k, _):
-        y_copy(k).wait_recv()
+        y_copy(5, k, y, near).wait_recv()
+        y_copy(6, k, 1 - y, near).wait_recv()
         for q in range(4):
-            out_ref[q, :, cols(k)] = y_s[k, q % 2, q // 2]
+            out_copy(k, q).start()
         return 0
 
     lax.fori_loop(0, chunks, out_step, 0)
 
     def sum_step(k, acc):
-        far_copy(7, k, n_chip, n_far).wait_recv()
-        val = n_part[k, c, y].astype(F32) + n_near[k, y].astype(F32) + n_far[k].astype(F32)
-        upper = val * gain_ref[:, cols(k)]
+        upper = own_sum(10, k, *n_bufs) * gain(k)
         dn_s[:, cols(k)] = upper
         return acc + jnp.sum(upper * xq[c, y, :, cols(k)], axis=-1, keepdims=True)
 
-    acc = lax.fori_loop(0, chunks, sum_step, jnp.zeros((quarter, 1), F32))
+    acc = lax.fori_loop(0, chunks, sum_step, zero)
     inv_own = inv_s[y * 2 + c]
     x_factor = inv_own * inv_own * inv_own * (acc / width)
 
     def grad_step(k, _):
         dx = inv_own * dn_s[:, cols(k)] - xq[c, y, :, cols(k)] * x_factor
-        grad_ref[:, cols(k)] = (dy_own[y, :, cols(k)] + dx).astype(BF16)
+        grad_ref[:, cols(k)] = (dy_own[:, cols(k)] + dx).astype(BF16)
         return 0
 
     lax.fori_loop(0, chunks, grad_step, 0)
 
     def drain(k, _):
-        near_copy(0, k, g_part, g_near).wait_send()
-        far_copy(1, k, g_chip, g_far).wait_send()
-        near_copy(2, k, b_part, b_near).wait_send()
-        far_copy(3, k, b_chip, b_far).wait_send()
-        y_copy(k).wait_send()
-        dy_copy(k).wait_send()
-        near_copy(6, k, n_part, n_near).wait_send()
-        far_copy(7, k, n_chip, n_far).wait_send()
+        for q in range(4):
+            out_copy(k, q).wait()
+        for kind, bufs in ((0, goal_bufs), (2, branch_bufs), (10, n_bufs)):
+            near_copy(kind, k, bufs[0], bufs[1]).wait_send()
+            far_copy(kind + 1, k, bufs[2], bufs[3]).wait_send()
+        for first, copy in ((4, y_copy), (7, dy_copy)):
+            copy(first, k, y, far).wait_send()
+            copy(first + 1, k, y, near).wait_send()
+            copy(first + 2, k, 1 - y, near).wait_send()
         return 0
 
     lax.fori_loop(0, chunks, drain, 0)
@@ -555,7 +589,10 @@
     vmem = pltpu.VMEM
     half = (k, 2, quarter, chunk)
     parts = (k, 2, 2, quarter, chunk)
+    own = (k, quarter, chunk)
     scratch = [
+        vmem((rows,), jnp.int32),
+        vmem((width,), F32),
         vmem((rows, depth), BF16),
         vmem((k, depth, chunk), BF16),
         vmem((rows, width), BF16),
@@ -570,32 +607,33 @@
         vmem((rows, heads), BF16),
         vmem(parts, BF16),
         vmem(half, BF16),
-        vmem(half, BF16),
-        vmem(half, BF16),
+        vmem(own, BF16),
+        vmem(own, BF16),
         vmem(parts, BF16),
         vmem(half, BF16),
-        vmem(half, BF16),
-        vmem(half, BF16),
-        vmem(half, F32),
+        vmem(own, BF16),
+        vmem(own, BF16),
+        vmem(own, F32),
         vmem(parts, BF16),
         vmem(parts, BF16),
-        vmem((2, quarter, width), F32),
+        vmem((quarter, width), F32),
         vmem((rows, heads), F32),
         vmem((rows, 2 * heads), BF16),
         vmem(parts, BF16),
         vmem(half, BF16),
-        vmem((k, quarter, chunk), BF16),
-        vmem((k, quarter, chunk), BF16),
+        vmem(own, BF16),
+        vmem(own, BF16),
         vmem((quarter, width), F32),
-        pltpu.SemaphoreType.DMA((5,)),
+        pltpu.SemaphoreType.DMA((7,)),
         pltpu.SemaphoreType.DMA((k,)),
-        pltpu.SemaphoreType.DMA((8, k)),
-        pltpu.SemaphoreType.DMA((8, k)),
+        pltpu.SemaphoreType.DMA((12, k)),
+        pltpu.SemaphoreType.DMA((12, k)),
         pltpu.SemaphoreType.DMA((2,)),
+        pltpu.SemaphoreType.DMA((k, 4)),
     ]
     smem = pl.BlockSpec(memory_space=pltpu.SMEM)
     in_vmem = pl.BlockSpec(memory_space=pltpu.VMEM)
-    anywhere = pl.BlockSpec(memory_space=pl.ANY)
+    in_hbm = pl.BlockSpec(memory_space=pltpu.HBM)
     flops = 2 * rows * width * (depth + 6 * heads)
     moved = 2 * width * (depth + 3 * heads + 3 * rows)
     student_out, grad_in = pl.pallas_call(
@@ -604,8 +642,8 @@
             jax.ShapeDtypeStruct((4, quarter, width), BF16),
             jax.ShapeDtypeStruct((quarter, width), BF16),
         ),
-        in_specs=[smem, smem, in_vmem, in_vmem] + [anywhere] * 6,
-        out_specs=(in_vmem, in_vmem),
+        in_specs=[smem, smem] + [in_hbm] * 8,
+        out_specs=(in_hbm, in_vmem),
         scratch_shapes=scratch,
         cost_estimate=pl.CostEstimate(flops=flops, bytes_accessed=moved, transcendentals=0),
         compiler_params=pltpu.CompilerParams(
@@ -614,8 +652,8 @@
     )(
         row_offsets,
         row_counts,
-        doc_start.reshape(1, rows),
-        norm_gain.reshape(1, width),
+        doc_start,
+        norm_gain,
         teacher_hidden,
         proj_weight,
         student_in,
@@ -626,7 +664,7 @@
     return (student_out.reshape(rows, width), grad_in)
 
 
-VMEM_BYTES = 52 * 2**20
+VMEM_BYTES = 60 * 2**20
 
 
 def solution(mesh):

time: 54.3 us -> 54.2 us (level)
  Pallas kernels: 48 us -> 49 us
  local copies, waits for them, and re-layouts: 4.07 us -> 3.09 us
    pallas_call x1, Pallas kernels: 48 us -> 49 us  [fused_body(): pl.pallas_call(functools.partial(step_kernel, lax.axis_size('seq')), out_...]
    reshape x1 -> x0, local copies, waits for them, and re-layouts: 0.73 us -> none  [fused_body(): norm_gain.reshape(1, width)]
    unnamed x6 -> x4, local copies, waits for them, and re-layouts: 3.34 us -> 3.09 us
where the time goes in v2:
time: 54.2 us; the launch traced here: 54.1 us
  Pallas kernels  49 us (90%)
  local copies, waits for them, and re-layouts  3.09 us (6%)
  between operations  1.94 us (4%)
    pallas_call x1, Pallas kernels, fused_body(): pl.pallas_call(functools.partial(step_kernel, lax.axis_size('seq')), out_...  49 us
    unnamed x4, local copies, waits for them, and re-layouts  3.09 us

profile of v2, /device:TPU:9, one launch (start us, length us, event | category | flops | bytes accessed | tf_op | source)
XLA Modules:
  0.0 54.1 jit_solution(18183970047971283502)
XLA Ops:
  1.9 49.0 %shard_map.113 = (bf16[4,40,3584]{2,1,0:T(8,128)(2,1)}, bf16[40,3584]{1,0:T(8,128)(2,1)}) custom-call(s32[1]{0:T(128)S(6)} %copy.14.offset_ref, s32[1]{0:T(128)S(6)} %copy.15.count_ref, s32[160]{0:T(256)} %start_hbm.1, f32[3584]{0:T(1024)} %gain_hbm.1, bf16[128,1024]{1,0:T(8,128)(2,1)} %teacher_hbm.1, bf16[1024,3584]{1,0:T(8,128)(2,1)} %proj_hbm.1, ...), custom_call_target="tpu_custom_call" | custom-call | flops 2936012800 | bytes 16285696 | tf_op jit(solution)/shard_map/pallas_call | solution.py:639
  51.0 0.0 copy-start
  51.0 2.4 %copy.16 = bf16[160,3584]{1,0:T(8,128)(2,1)} copy(bf16[160,3584]{1,0:T(8,128)(2,1)} %bitcast.1) | data formatting | bytes 2293760
  53.3 0.0 copy-done
  53.3 0.7 %copy.17 = bf16[40,3584]{1,0:T(8,128)(2,1)} copy(bf16[40,3584]{1,0:T(8,128)(2,1)S(1)} %copy-done) | data formatting | bytes 573440
Async XLA Ops:
  51.0 2.4 %copy-start = (bf16[40,3584]{1,0:T(8,128)(2,1)S(1)}, bf16[40,3584]{1,0:T(8,128)(2,1)}, u32[]{:S(2)}) copy-start(bf16[40,3584]{1,0:T(8,128)(2,1)} %get-tuple-element.9) | copy-start | bytes 860164

commit v3 on v2

--- a/solution.py
+++ b/solution.py
@@ -217,6 +217,18 @@
     far = {"tp": (1 - y) * 2 + c}
     scale = 1.0 / math.sqrt(HD)
 
+    barrier = pltpu.get_barrier_semaphore()
+    pl.semaphore_signal(barrier, inc=1, device_id=near, device_id_type=MESH)
+    pl.semaphore_signal(barrier, inc=1, device_id=far, device_id_type=MESH)
+
+    @pl.when(s > 0)
+    def _():
+        pl.semaphore_signal(barrier, inc=1, device_id={"seq": s - 1}, device_id_type=MESH)
+
+    @pl.when(s < n_seq - 1)
+    def _():
+        pl.semaphore_signal(barrier, inc=1, device_id={"seq": s + 1}, device_id_type=MESH)
+
     def gain(k):
         return gain_s[cols(k)][None, :]
 
@@ -237,8 +249,8 @@
             ]
         )
     ]
-    loads[3].start()
-    loads[0].start()
+    for i in (0, 6, 3, 1):
+        loads[i].start()
 
     def proj_load(k):
         return pltpu.make_async_copy(proj_hbm.at[:, cols(k)], proj.at[k], proj_sem.at[k])
@@ -248,20 +260,21 @@
         return 0
 
     lax.fori_loop(0, chunks, start_proj, 0)
-    for i in (1, 2, 6, 5, 4):
+    for i in (2, 5, 4):
         loads[i].start()
 
-    barrier = pltpu.get_barrier_semaphore()
-    pl.semaphore_signal(barrier, inc=1, device_id=near, device_id_type=MESH)
-    pl.semaphore_signal(barrier, inc=1, device_id=far, device_id_type=MESH)
-
-    @pl.when(s > 0)
-    def _():
-        pl.semaphore_signal(barrier, inc=1, device_id={"seq": s - 1}, device_id_type=MESH)
-
-    @pl.when(s < n_seq - 1)
-    def _():
-        pl.semaphore_signal(barrier, inc=1, device_id={"seq": s + 1}, device_id_type=MESH)
+    loads[0].wait()
+
+    def square(k, acc):
+        v = x_in[:, cols(k)].astype(F32)
+        for q in range(4):
+            xq[q % 2, q // 2, :, cols(k)] = v[q * quarter : (q + 1) * quarter]
+        return acc + jnp.sum(v * v, axis=1, keepdims=True)
+
+    total = lax.fori_loop(0, chunks, square, jnp.zeros((rows, 1), F32))
+    inv = lax.rsqrt(total / width + epsilon)
+    for q in range(4):
+        inv_s[q] = inv[q * quarter : (q + 1) * quarter]
 
     inner = (s > 0) & (s < n_seq - 1)
 
@@ -305,18 +318,17 @@
         for q in range(4):
             ref[k, q % 2, q // 2] = val[q * quarter : (q + 1) * quarter].astype(BF16)
 
-    loads[0].wait()
-
-    def square(k, acc):
+    loads[6].wait()
+
+    def norm(k, _):
         v = x_in[:, cols(k)].astype(F32)
-        for q in range(4):
-            xq[q % 2, q // 2, :, cols(k)] = v[q * quarter : (q + 1) * quarter]
-        return acc + jnp.sum(v * v, axis=1, keepdims=True)
-
-    total = lax.fori_loop(0, chunks, square, jnp.zeros((rows, 1), F32))
-    inv = lax.rsqrt(total / width + epsilon)
-    for q in range(4):
-        inv_s[q] = inv[q * quarter : (q + 1) * quarter]
+        normed[:, cols(k)] = (v * inv * gain(k)).astype(BF16)
+        return 0
+
+    lax.fori_loop(0, chunks, norm, 0)
+
+    loads[1].wait()
+    qkv[:, 0 : QPK * HD] = dot(normed[...], wq[...]).astype(BF16)
 
     start = offset_ref[0] - s * own_tokens + shift
     r_i = lax.broadcasted_iota(jnp.int32, (rows, rows), 0)
@@ -373,18 +385,7 @@
 
     goal_bufs = (g_part, g_near, g_chip, g_far)
     scatter(0, project, *goal_bufs)
-    loads[6].wait()
-
-    def norm(k, _):
-        v = x_in[:, cols(k)].astype(F32)
-        normed[:, cols(k)] = (v * inv * gain(k)).astype(BF16)
-        return 0
-
-    lax.fori_loop(0, chunks, norm, 0)
-
-    loads[1].wait()
     loads[2].wait()
-    qkv[:, 0 : QPK * HD] = dot(normed[...], wq[...]).astype(BF16)
     scatter_rest(0, *goal_bufs)
     qkv[:, QPK * HD :] = dot(normed[...], wkv[...]).astype(BF16)
     loads[5].wait()
@@ -526,26 +527,8 @@
 
     lax.fori_loop(0, chunks, out_step, 0)
 
-    def sum_step(k, acc):
-        upper = own_sum(10, k, *n_bufs) * gain(k)
-        dn_s[:, cols(k)] = upper
-        return acc + jnp.sum(upper * xq[c, y, :, cols(k)], axis=-1, keepdims=True)
-
-    acc = lax.fori_loop(0, chunks, sum_step, zero)
-    inv_own = inv_s[y * 2 + c]
-    x_factor = inv_own * inv_own * inv_own * (acc / width)
-
-    def grad_step(k, _):
-        dx = inv_own * dn_s[:, cols(k)] - xq[c, y, :, cols(k)] * x_factor
-        grad_ref[:, cols(k)] = (dy_own[:, cols(k)] + dx).astype(BF16)
-        return 0
-
-    lax.fori_loop(0, chunks, grad_step, 0)
-
-    def drain(k, _):
-        for q in range(4):
-            out_copy(k, q).wait()
-        for kind, bufs in ((0, goal_bufs), (2, branch_bufs), (10, n_bufs)):
+    def drain_early(k, _):
+        for kind, bufs in ((0, goal_bufs), (2, branch_bufs)):
             near_copy(kind, k, bufs[0], bufs[1]).wait_send()
             far_copy(kind + 1, k, bufs[2], bufs[3]).wait_send()
         for first, copy in ((4, y_copy), (7, dy_copy)):
@@ -554,11 +537,45 @@
             copy(first + 2, k, 1 - y, near).wait_send()
         return 0
 
-    lax.fori_loop(0, chunks, drain, 0)
+    lax.fori_loop(0, chunks, drain_early, 0)
 
     @pl.when(s < n_seq - 1)
     def _():
         shift_copy(s + 1).wait_send()
+
+    def sum_step(k, acc):
+        upper = own_sum(10, k, *n_bufs) * gain(k)
+        dn_s[:, cols(k)] = upper
+        return acc + jnp.sum(upper * xq[c, y, :, cols(k)], axis=-1, keepdims=True)
+
+    acc = lax.fori_loop(0, chunks, sum_step, zero)
+    inv_own = inv_s[y * 2 + c]
+    x_factor = inv_own * inv_own * inv_own * (acc / width)
+
+    def grad_step(k, _):
+        dx = inv_own * dn_s[:, cols(k)] - xq[c, y, :, cols(k)] * x_factor
+        grad_ref[:, cols(k)] = (dy_own[:, cols(k)] + dx).astype(BF16)
+        return 0
+
+    lax.fori_loop(0, chunks, grad_step, 0)
+
+    def drain(k, _):
+        for q in range(4):
+            out_copy(k, q).wait()
+        near_copy(10, k, n_part, n_near).wait_send()
+        far_copy(11, k, n_chip, n_far).wait_send()
+        return 0
+
+    lax.fori_loop(0, chunks, drain, 0)
+
+
+def hand_over(y_ref, g_ref, out_ref, grad_ref, sem):
+    copies = [pltpu.make_async_copy(y_ref.at[q], out_ref.at[q], sem.at[q]) for q in range(4)]
+    copies.append(pltpu.make_async_copy(g_ref, grad_ref, sem.at[4]))
+    for one in copies:
+        one.start()
+    for one in copies:
+        one.wait()
 
 
 def chunk_of(width):
@@ -661,6 +678,17 @@
         w_keyval,
         w_out,
     )
+    student_out, grad_in = pl.pallas_call(
+        hand_over,
+        out_shape=(
+            jax.ShapeDtypeStruct(student_out.shape, BF16),
+            jax.ShapeDtypeStruct(grad_in.shape, BF16),
+        ),
+        in_specs=[in_hbm, in_hbm],
+        out_specs=(in_hbm, in_hbm),
+        scratch_shapes=[pltpu.SemaphoreType.DMA((5,))],
+        compiler_params=pltpu.CompilerParams(vmem_limit_bytes=VMEM_BYTES),
+    )(student_out, grad_in)
     return (student_out.reshape(rows, width), grad_in)
 
 

time: 54.2 us -> 96.1 us (1.77)
  Pallas kernels: 49 us -> 94 us
  local copies, waits for them, and re-layouts: 3.09 us -> 0 us
    pallas_call x0 -> x1, Pallas kernels: none -> 44.6 us  [fused_body(): pl.pallas_call(hand_over, out_shape=(jax.ShapeDtypeStruct(student_out.sha...]
    unnamed x4 -> x0, local copies, waits for them, and re-layouts: 3.09 us -> none
where the time goes in v3:
time: 96.1 us; the launch traced here: 96 us
  Pallas kernels  94 us (98%)
  between operations  1.93 us (2%)
    pallas_call x1, Pallas kernels, fused_body(): pl.pallas_call(functools.partial(step_kernel, lax.axis_size('seq')), out_...  49.5 us
    pallas_call x1, Pallas kernels, fused_body(): pl.pallas_call(hand_over, out_shape=(jax.ShapeDtypeStruct(student_out.sha...  44.6 us

profile of v3, /device:TPU:9, one launch (start us, length us, event | category | flops | bytes accessed | tf_op | source)
XLA Modules:
  0.0 96.0 jit_solution(18229399289287079606)
XLA Ops:
  1.9 49.5 %shard_map.113 = (bf16[4,40,3584]{2,1,0:T(8,128)(2,1)}, bf16[40,3584]{1,0:T(8,128)(2,1)}) custom-call(s32[1]{0:T(128)S(6)} %copy.12.offset_ref, s32[1]{0:T(128)S(6)} %copy.13.count_ref, s32[160]{0:T(256)} %start_hbm.1, f32[3584]{0:T(1024)} %gain_hbm.1, bf16[128,1024]{1,0:T(8,128)(2,1)} %teacher_hbm.1, bf16[1024,3584]{1,0:T(8,128)(2,1)} %proj_hbm.1, ...), custom_call_target="tpu_custom_call" | custom-call | flops 2936012800 | bytes 16285696 | tf_op jit(solution)/shard_map/pallas_call | solution.py:656
  51.4 44.6 %shard_map.114 = (bf16[4,40,3584]{2,1,0:T(8,128)(2,1)}, bf16[40,3584]{1,0:T(8,128)(2,1)}) custom-call(bf16[4,40,3584]{2,1,0:T(8,128)(2,1)} %get-tuple-element.6.y_ref, bf16[40,3584]{1,0:T(8,128)(2,1)} %get-tuple-element.7.g_ref), custom_call_target="tpu_custom_call" | custom-call | tf_op jit(solution)/shard_map/pallas_call | solution.py:681

commit v4 on v3

--- a/solution.py
+++ b/solution.py
@@ -433,7 +433,7 @@
 
     zero = jnp.zeros((quarter, 1), F32)
     asum, bsum, both_sum = lax.fori_loop(0, chunks, loss_step, (zero, zero, zero))
-    early = min(2, chunks)
+    early = min(3, chunks)
 
     def start_y(k, _):
         y_copy(4, k, y, far).start()
@@ -569,12 +569,17 @@
     lax.fori_loop(0, chunks, drain, 0)
 
 
-def hand_over(y_ref, g_ref, out_ref, grad_ref, sem):
-    copies = [pltpu.make_async_copy(y_ref.at[q], out_ref.at[q], sem.at[q]) for q in range(4)]
-    copies.append(pltpu.make_async_copy(g_ref, grad_ref, sem.at[4]))
-    for one in copies:
+def hand_over(y_ref, g_ref, out_ref, grad_ref, y_buf, g_buf, in_sem, out_sem):
+    spans = [(y_ref.at[q], y_buf.at[q], out_ref.at[q]) for q in range(4)]
+    spans.append((g_ref, g_buf, grad_ref))
+    inward = [pltpu.make_async_copy(a, b, in_sem.at[i]) for i, (a, b, _) in enumerate(spans)]
+    outward = [pltpu.make_async_copy(b, a, out_sem.at[i]) for i, (_, b, a) in enumerate(spans)]
+    for one in inward:
         one.start()
-    for one in copies:
+    for one, then in zip(inward, outward):
+        one.wait()
+        then.start()
+    for one in outward:
         one.wait()
 
 
@@ -686,7 +691,12 @@
         ),
         in_specs=[in_hbm, in_hbm],
         out_specs=(in_hbm, in_hbm),
-        scratch_shapes=[pltpu.SemaphoreType.DMA((5,))],
+        scratch_shapes=[
+            vmem(student_out.shape, BF16),
+            vmem(grad_in.shape, BF16),
+            pltpu.SemaphoreType.DMA((5,)),
+            pltpu.SemaphoreType.DMA((5,)),
+        ],
         compiler_params=pltpu.CompilerParams(vmem_limit_bytes=VMEM_BYTES),
     )(student_out, grad_in)
     return (student_out.reshape(rows, width), grad_in)

time: 96.1 us -> 53.7 us (0.56)
  Pallas kernels: 94 us -> 51.6 us
    pallas_call x1, Pallas kernels: 44.6 us -> 2.13 us  [fused_body(): pl.pallas_call(hand_over, out_shape=(jax.ShapeDtypeStruct(student_out.sha...]
where the time goes in v4:
time: 53.7 us; the launch traced here: 53.5 us
  Pallas kernels  51.6 us (96%)
  between operations  1.93 us (4%)
    pallas_call x1, Pallas kernels, fused_body(): pl.pallas_call(functools.partial(step_kernel, lax.axis_size('seq')), out_...  49.5 us
    pallas_call x1, Pallas kernels, fused_body(): pl.pallas_call(hand_over, out_shape=(jax.ShapeDtypeStruct(student_out.sha...  2.13 us

profile of v4, /device:TPU:9, one launch (start us, length us, event | category | flops | bytes accessed | tf_op | source)
XLA Modules:
  0.0 53.5 jit_solution(888124139868644796)
XLA Ops:
  1.9 49.5 %shard_map.113 = (bf16[4,40,3584]{2,1,0:T(8,128)(2,1)}, bf16[40,3584]{1,0:T(8,128)(2,1)}) custom-call(s32[1]{0:T(128)S(6)} %copy.12.offset_ref, s32[1]{0:T(128)S(6)} %copy.13.count_ref, s32[160]{0:T(256)} %start_hbm.1, f32[3584]{0:T(1024)} %gain_hbm.1, bf16[128,1024]{1,0:T(8,128)(2,1)} %teacher_hbm.1, bf16[1024,3584]{1,0:T(8,128)(2,1)} %proj_hbm.1, ...), custom_call_target="tpu_custom_call" | custom-call | flops 2936012800 | bytes 16285696 | tf_op jit(solution)/shard_map/pallas_call | solution.py:661
  51.4 2.1 %shard_map.114 = (bf16[4,40,3584]{2,1,0:T(8,128)(2,1)}, bf16[40,3584]{1,0:T(8,128)(2,1)}) custom-call(bf16[4,40,3584]{2,1,0:T(8,128)(2,1)} %get-tuple-element.6.y_ref, bf16[40,3584]{1,0:T(8,128)(2,1)} %get-tuple-element.7.g_ref), custom_call_target="tpu_custom_call" | custom-call | tf_op jit(solution)/shard_map/pallas_call | solution.py:686

commit v5 on v4

--- a/solution.py
+++ b/solution.py
@@ -138,6 +138,14 @@
 
 
 MESH = pl.DeviceIdType.MESH
+
+
+def unrolled(count, step, carry):
+    for k in range(count):
+        carry = step(k, carry)
+    return carry
+
+
 NT = (((1,), (1,)), ((), ()))
 TN = (((0,), (0,)), ((), ()))
 F32 = jnp.float32
@@ -233,6 +241,8 @@
         return gain_s[cols(k)][None, :]
 
     def cols(k):
+        if isinstance(k, int):
+            return pl.ds(k * chunk, chunk)
         return pl.ds(pl.multiple_of(k * chunk, chunk), chunk)
 
     loads = [
@@ -271,7 +281,7 @@
             xq[q % 2, q // 2, :, cols(k)] = v[q * quarter : (q + 1) * quarter]
         return acc + jnp.sum(v * v, axis=1, keepdims=True)
 
-    total = lax.fori_loop(0, chunks, square, jnp.zeros((rows, 1), F32))
+    total = unrolled(chunks, square, jnp.zeros((rows, 1), F32))
     inv = lax.rsqrt(total / width + epsilon)
     for q in range(4):
         inv_s[q] = inv[q * quarter : (q + 1) * quarter]
@@ -325,7 +335,7 @@
         normed[:, cols(k)] = (v * inv * gain(k)).astype(BF16)
         return 0
 
-    lax.fori_loop(0, chunks, norm, 0)
+    unrolled(chunks, norm, 0)
 
     loads[1].wait()
     qkv[:, 0 : QPK * HD] = dot(normed[...], wq[...]).astype(BF16)
@@ -348,10 +358,13 @@
     def far_copy(kind, k, chip, land):
         return remote(kind, k, chip.at[k], land.at[k], far)
 
+    def add_pair(k, part, land, chip):
+        pair = part[k, c, 1 - y].astype(F32) + land[k, 1 - y].astype(F32)
+        chip[k] = pair.astype(BF16)
+
     def pass_on(kind, k, part, land, chip, far_land):
         near_copy(kind, k, part, land).wait_recv()
-        pair = part[k, c, 1 - y].astype(F32) + land[k, 1 - y].astype(F32)
-        chip[k] = pair.astype(BF16)
+        add_pair(k, part, land, chip)
         far_copy(kind + 1, k, chip, far_land).start()
 
     def own_sum(kind, k, part, land, chip, far_land):
@@ -363,17 +376,17 @@
     lag = min(2, chunks)
 
     def scatter(kind, make, part, land, chip, far_land):
-        def step(k, _):
-            split_store(part, k, make(k))
+        for k in range(chunks):
+            behind = k - lag
+            if behind >= 0:
+                near_copy(kind, behind, part, land).wait_recv()
+            val = make(k)
+            if behind >= 0:
+                add_pair(behind, part, land, chip)
+            split_store(part, k, val)
             near_copy(kind, k, part, land).start()
-
-            @pl.when(k >= lag)
-            def _():
-                pass_on(kind, k - lag, part, land, chip, far_land)
-
-            return 0
-
-        lax.fori_loop(0, chunks, step, 0)
+            if behind >= 0:
+                far_copy(kind + 1, behind, chip, far_land).start()
 
     def scatter_rest(kind, part, land, chip, far_land):
         for k in range(chunks - lag, chunks):
@@ -432,7 +445,7 @@
         )
 
     zero = jnp.zeros((quarter, 1), F32)
-    asum, bsum, both_sum = lax.fori_loop(0, chunks, loss_step, (zero, zero, zero))
+    asum, bsum, both_sum = unrolled(chunks, loss_step, (zero, zero, zero))
     early = min(3, chunks)
 
     def start_y(k, _):
@@ -457,7 +470,7 @@
         dy_own[:, cols(k)] = dy
         return 0
 
-    lax.fori_loop(0, chunks, dy_step, 0)
+    unrolled(chunks, dy_step, 0)
 
     d_attn_s[...] = jnp.zeros_like(d_attn_s)
 
@@ -473,13 +486,12 @@
         dy_copy(7, k, y, far).wait_recv()
         dy_copy(9, k, 1 - y, near).start()
 
-        @pl.when(k > 0)
-        def _():
+        if k > 0:
             d_attn_part(k - 1)
 
         return 0
 
-    lax.fori_loop(0, chunks, d_attn_step, 0)
+    unrolled(chunks, d_attn_step, 0)
     lax.fori_loop(early, chunks, start_y, 0)
     d_attn_part(chunks - 1)
 
@@ -548,7 +560,7 @@
         dn_s[:, cols(k)] = upper
         return acc + jnp.sum(upper * xq[c, y, :, cols(k)], axis=-1, keepdims=True)
 
-    acc = lax.fori_loop(0, chunks, sum_step, zero)
+    acc = unrolled(chunks, sum_step, zero)
     inv_own = inv_s[y * 2 + c]
     x_factor = inv_own * inv_own * inv_own * (acc / width)
 
@@ -557,7 +569,7 @@
         grad_ref[:, cols(k)] = (dy_own[:, cols(k)] + dx).astype(BF16)
         return 0
 
-    lax.fori_loop(0, chunks, grad_step, 0)
+    unrolled(chunks, grad_step, 0)
 
     def drain(k, _):
         for q in range(4):

time: 53.7 us -> 53.5 us (level)
  no operation moved by 1% of the time
where the time goes in v5:
time: 53.5 us; the launch traced here: 53.3 us
  Pallas kernels  51.3 us (96%)
  between operations  1.93 us (4%)
    pallas_call x1, Pallas kernels, fused_body(): pl.pallas_call(functools.partial(step_kernel, lax.axis_size('seq')), out_...  49.2 us
    pallas_call x1, Pallas kernels, fused_body(): pl.pallas_call(hand_over, out_shape=(jax.ShapeDtypeStruct(student_out.sha...  2.13 us

profile of v5, /device:TPU:9, one launch (start us, length us, event | category | flops | bytes accessed | tf_op | source)
XLA Modules:
  0.0 53.3 jit_solution(14978181151232821126)
XLA Ops:
  1.9 49.2 %shard_map.113 = (bf16[4,40,3584]{2,1,0:T(8,128)(2,1)}, bf16[40,3584]{1,0:T(8,128)(2,1)}) custom-call(s32[1]{0:T(128)S(6)} %copy.12.offset_ref, s32[1]{0:T(128)S(6)} %copy.13.count_ref, s32[160]{0:T(256)} %start_hbm.1, f32[3584]{0:T(1024)} %gain_hbm.1, bf16[128,1024]{1,0:T(8,128)(2,1)} %teacher_hbm.1, bf16[1024,3584]{1,0:T(8,128)(2,1)} %proj_hbm.1, ...), custom_call_target="tpu_custom_call" | custom-call | flops 2936012800 | bytes 16285696 | tf_op jit(solution)/shard_map/pallas_call | solution.py:673
  51.1 2.1 %shard_map.114 = (bf16[4,40,3584]{2,1,0:T(8,128)(2,1)}, bf16[40,3584]{1,0:T(8,128)(2,1)}) custom-call(bf16[4,40,3584]{2,1,0:T(8,128)(2,1)} %get-tuple-element.6.y_ref, bf16[40,3584]{1,0:T(8,128)(2,1)} %get-tuple-element.7.g_ref), custom_call_target="tpu_custom_call" | custom-call | tf_op jit(solution)/shard_map/pallas_call | solution.py:698

commit v6 on v5

--- a/solution.py
+++ b/solution.py
@@ -373,7 +373,7 @@
             part[k, c, y].astype(F32) + land[k, y].astype(F32) + far_land[k].astype(F32)
         )
 
-    lag = min(2, chunks)
+    lag = min(1, chunks)
 
     def scatter(kind, make, part, land, chip, far_land):
         for k in range(chunks):

time: 53.5 us -> 61.2 us (1.14)
  Pallas kernels: 51.3 us -> 58.5 us
    pallas_call x1, Pallas kernels: 49.2 us -> 56.4 us  [fused_body(): pl.pallas_call(functools.partial(step_kernel, lax.axis_size('seq')), out_...]
where the time goes in v6:
time: 61.2 us; the launch traced here: 60.4 us
  Pallas kernels  58.5 us (96%)
  between operations  1.93 us (3%)
    pallas_call x1, Pallas kernels, fused_body(): pl.pallas_call(functools.partial(step_kernel, lax.axis_size('seq')), out_...  56.4 us
    pallas_call x1, Pallas kernels, fused_body(): pl.pallas_call(hand_over, out_shape=(jax.ShapeDtypeStruct(student_out.sha...  2.13 us

profile of v6, /device:TPU:9, one launch (start us, length us, event | category | flops | bytes accessed | tf_op | source)
XLA Modules:
  0.0 60.4 jit_solution(10016338364041727848)
XLA Ops:
  1.9 56.4 %shard_map.113 = (bf16[4,40,3584]{2,1,0:T(8,128)(2,1)}, bf16[40,3584]{1,0:T(8,128)(2,1)}) custom-call(s32[1]{0:T(128)S(6)} %copy.12.offset_ref, s32[1]{0:T(128)S(6)} %copy.13.count_ref, s32[160]{0:T(256)} %start_hbm.1, f32[3584]{0:T(1024)} %gain_hbm.1, bf16[128,1024]{1,0:T(8,128)(2,1)} %teacher_hbm.1, bf16[1024,3584]{1,0:T(8,128)(2,1)} %proj_hbm.1, ...), custom_call_target="tpu_custom_call" | custom-call | flops 2936012800 | bytes 16285696 | tf_op jit(solution)/shard_map/pallas_call | solution.py:673
  58.3 2.1 %shard_map.114 = (bf16[4,40,3584]{2,1,0:T(8,128)(2,1)}, bf16[40,3584]{1,0:T(8,128)(2,1)}) custom-call(bf16[4,40,3584]{2,1,0:T(8,128)(2,1)} %get-tuple-element.6.y_ref, bf16[40,3584]{1,0:T(8,128)(2,1)} %get-tuple-element.7.g_ref), custom_call_target="tpu_custom_call" | custom-call | tf_op jit(solution)/shard_map/pallas_call | solution.py:698
